TPU v7x, 512 devices: a whole 4x4x16 slice. The times are simulated.
512 devices in a mesh: head: 8 (over z_lo), blk: 32 (over z_hi, x, y), enc: 2 (over core).
Axes of the slice: x: 4, y: 4, z: 16 (z_hi: 2, z_lo: 8; z = z_hi * 8 + z_lo), core: 2. Of those that a mesh axis runs over, the one named last changes fastest.
Arguments:
- queries: bfloat16 [32, 896, 5120], P('blk', ('head', 'enc')), may hold values from -30 to 30
- key_rows: bfloat16 [32, 896, 5120], P('blk', ('head', 'enc')), may hold values from -30 to 30
- value_rows: bfloat16 [32, 896, 5120], P('blk', ('head', 'enc')), may hold values from -6 to 6
- text_queries: bfloat16 [32, 896, 5120], P('blk', ('head', 'enc')), may hold values from -300 to 300
- prompt_embed: bfloat16 [512, 4096], P('enc', 'blk'), may hold values from -6 to 6
- key_weight: bfloat16 [4096, 5120], P('blk', 'head'), may hold values from -0.09375 to 0.09375
- value_weight: bfloat16 [4096, 5120], P('blk', 'head'), may hold values from -0.09375 to 0.09375
- stop_count: int32 [32], P('blk'), may hold values from 1 to 3, as said below
- prompt_length: int32 [1], replicated, may hold values from 64 to 512
Outputs:
- mixed: bfloat16 [32, 896, 5120], P('blk', ('head', 'enc'))
Inputs may be any that keep to these rules, and one draw needn't show every extreme that they name: `stop_count`: some block sees all 3 blocks.
All inputs are finite; a program needn't handle non-finite values.
Results may differ from a plain program's by a relative error of at most 0.0083.
Values may be sent and summed in bfloat16 or wider, within the bound.
A program may use at most 64 MiB of HBM per device.

v0:
```python
import jax
import jax.numpy as jnp
from jax import lax
from jax.sharding import PartitionSpec as P

HEAD_DIM = 128
STOPS = 3


def passed_along(value, axis, steps):
    count = lax.axis_size(axis)
    pairs = [(source, (source + steps) % count) for source in range(count)]
    return lax.ppermute(value, axis, pairs)


def head_attention(head_query, known_keys, known_values, allowed):
    scores = jnp.einsum(
        "qd,kd->qk", head_query, known_keys, preferred_element_type=jnp.float32
    ) * float(HEAD_DIM) ** (-0.5)
    scores = jnp.where(allowed[None, :], scores, jnp.float32(-1e30))
    row_peak = jnp.max(scores, axis=1, keepdims=True)
    weights = jnp.where(allowed[None, :], jnp.exp(scores - row_peak), jnp.float32(0.0))
    weight_sum = jnp.sum(weights, axis=1, keepdims=True)
    rounded = weights.astype(jnp.bfloat16)
    return jnp.dot(rounded, known_values, preferred_element_type=jnp.float32) / weight_sum


def by_heads(matrix):
    return jnp.transpose(matrix.reshape(matrix.shape[0], -1, HEAD_DIM), (1, 0, 2))


def body(
    queries,
    key_rows,
    value_rows,
    text_queries,
    prompt_embed,
    key_weight,
    value_weight,
    stop_count,
    prompt_length,
):
    local_query, local_keys, local_values, local_cross = (
        lax.all_to_all(queries[0], "head", split_axis=1, concat_axis=0, tiled=True),
        lax.all_to_all(key_rows[0], "head", split_axis=1, concat_axis=0, tiled=True),
        lax.all_to_all(value_rows[0], "head", split_axis=1, concat_axis=0, tiled=True),
        lax.all_to_all(text_queries[0], "head", split_axis=1, concat_axis=0, tiled=True),
    )
    key_part = jnp.dot(prompt_embed, key_weight, preferred_element_type=jnp.float32)
    value_part = jnp.dot(prompt_embed, value_weight, preferred_element_type=jnp.float32)
    key_total, value_total = lax.psum((key_part, value_part), "blk")
    text_keys, text_values = (
        lax.all_gather(key_total.astype(jnp.bfloat16), "enc", axis=0, tiled=True),
        lax.all_gather(value_total.astype(jnp.bfloat16), "enc", axis=0, tiled=True),
    )
    stacked = jnp.stack([local_keys, local_values])
    source = lax.all_gather(stacked, "enc", axis=1, tiled=True)
    seen_blocks = [source]
    moving = source
    for offset in range(1, STOPS):
        moving = passed_along(moving, "blk", 1)
        seen_blocks.append(moving)
    near_pairs = jnp.concatenate(seen_blocks, axis=1)
    block_span = seen_blocks[0].shape[1]
    allowed = jnp.repeat(jnp.arange(STOPS, dtype=jnp.int32) < stop_count[0], block_span)
    text_live = jnp.arange(text_keys.shape[0], dtype=jnp.int32) < prompt_length[0]

    def one_head(items):
        head_query, head_keys, head_values, head_cross, cross_keys, cross_values = items
        self_out = head_attention(head_query, head_keys, head_values, allowed)
        cross_out = head_attention(head_cross, cross_keys, cross_values, text_live)
        return (self_out + cross_out).astype(jnp.bfloat16)

    result = lax.map(
        one_head,
        (
            by_heads(local_query),
            by_heads(near_pairs[0]),
            by_heads(near_pairs[1]),
            by_heads(local_cross),
            by_heads(text_keys),
            by_heads(text_values),
        ),
    )
    token_major = jnp.transpose(result, (1, 0, 2)).reshape(local_query.shape[0], -1)
    returned = lax.all_to_all(token_major, "head", split_axis=0, concat_axis=1, tiled=True)
    return returned[None]


def solution(mesh):
    placed = (
        P("blk", ("head", "enc"), None),
        P("blk", ("head", "enc"), None),
        P("blk", ("head", "enc"), None),
        P("blk", ("head", "enc"), None),
        P("enc", "blk"),
        P("blk", "head"),
        P("blk", "head"),
        P("blk"),
        P(),
    )
    return jax.shard_map(
        body, mesh=mesh, in_specs=placed, out_specs=P("blk", ("head", "enc"), None), check_vma=False
    )
```

profile of v0, /device:TPU:1, one launch (start us, length us, event | category | flops | bytes accessed | tf_op | source)
XLA Modules:
  0.0 996.7 jit_solution(15385562048824078471)
XLA Ops:
  6.5 1.2 copy.62
  7.7 0.9 copy.42
  8.6 13.1 %all-to-all-start.1 = ((bf16[56,8,640]{2,0,1:T(8,128)(2,1)}), bf16[56,8,640]{2,0,1:T(8,128)(2,1)S(1)}, u32[]{:S(2)}, u32[]{:S(2)}) async-start(bf16[56,8,640]{2,0,1:T(8,128)(2,1)} %copy.42), calls=%async_computation.1 | async-start | bytes 1146880 | tf_op jit(solution)/shard_map/all_to_all | solution.py:45
  21.7 1.1 copy.63
  22.9 21.0 %all-to-all-done.1 = bf16[56,8,640]{2,0,1:T(8,128)(2,1)S(1)} async-done(((bf16[56,8,640]{2,0,1:T(8,128)(2,1)}), bf16[56,8,640]{2,0,1:T(8,128)(2,1)S(1)}, u32[]{:S(2)}, u32[]{:S(2)}) %all-to-all-start.1) | async-done | bytes 573472 | tf_op jit(solution)/shard_map/all_to_all | solution.py:45
  43.9 41.4 %all_to_all.80 = bf16[56,8,640]{2,0,1:T(8,128)(2,1)S(1)} all-to-all(bf16[56,8,640]{2,0,1:T(8,128)(2,1)S(1)} %copy.43), channel_id=1, replica_groups=mesh['head'=8,'blk'=32,'enc'=2] {'head'}, dimensions={1} | all-to-all | bytes 1146880 | tf_op jit(solution)/shard_map/all_to_all | solution.py:46
  85.2 1.1 pad_maximum_fusion
  86.4 22.0 %all-gather.2.cloned.1.call-done = bf16[2,896,640]{2,1,0:T(8,128)(2,1)} async-done(((bf16[2,448,640]{2,1,0:T(8,128)(2,1)}), bf16[2,896,640]{2,1,0:T(8,128)(2,1)}) %all-gather.2.cloned.1.call-update) | async-done | bytes 2293776 | tf_op jit(solution)/shard_map/all_gather | solution.py:57
  108.4 2.1 collective-permute-start
  110.6 0.9 copy.41
  111.5 9.7 all-to-all-start
  121.3 0.9 copy.46
  122.2 21.9 %all-to-all-done = bf16[56,8,640]{2,0,1:T(8,128)(2,1)S(1)} async-done(((bf16[56,8,640]{2,0,1:T(8,128)(2,1)}), bf16[56,8,640]{2,0,1:T(8,128)(2,1)S(1)}, u32[]{:S(2)}, u32[]{:S(2)}) %all-to-all-start) | async-done | bytes 573472 | tf_op jit(solution)/shard_map/all_to_all | solution.py:44
  144.0 12.3 %all-to-all-start.3 = ((bf16[56,8,640]{2,0,1:T(8,128)(2,1)}), bf16[56,8,640]{2,0,1:T(8,128)(2,1)S(1)}, u32[]{:S(2)}, u32[]{:S(2)}) async-start(bf16[56,8,640]{2,0,1:T(8,128)(2,1)} %copy.46), calls=%async_computation.3 | async-start | bytes 1146880 | tf_op jit(solution)/shard_map/all_to_all | solution.py:47
  156.3 153.2 %collective-permute-done = bf16[2,896,640]{2,1,0:T(8,128)(2,1)} collective-permute-done((bf16[2,896,640]{2,1,0:T(8,128)(2,1)}, bf16[2,896,640]{2,1,0:T(8,128)(2,1)}, u32[]{:S(2)}, u32[]{:S(2)}) %collective-permute-start) | collective-permute-done | bytes 2293792 | tf_op jit(solution)/shard_map/ppermute | solution.py:13
  309.6 1.9 collective-permute-start.1
  312.0 508.5 %all-reduce.2 = (bf16[256,640]{1,0:T(8,128)(2,1)S(1)}, bf16[256,640]{1,0:T(8,128)(2,1)S(1)}) all-reduce(f32[256,640]{1,0:T(8,128)S(1)} %fusion.46, f32[256,640]{1,0:T(8,128)S(1)} %fusion.47), channel_id=1, replica_groups=mesh['head'=8,'blk'=32,'enc'=2] {'blk'}, use_global_device_ids=true, to_apply=%region_0.0 | all-reduce | flops 327680 | bytes 1966080 | tf_op jit(solution)/shard_map/psum | solution.py:51
  820.5 16.5 %all_gather.10 = bf16[512,640]{1,0:T(8,128)(2,1)S(1)} all-gather(bf16[256,640]{1,0:T(8,128)(2,1)S(1)} %get-tuple-element.133), channel_id=1, replica_groups=mesh['head'=8,'blk'=32,'enc'=2] {'enc'}, dimensions={0}, use_global_device_ids=true | all-gather | bytes 983040 | tf_op jit(solution)/shard_map/all_gather | solution.py:53
  837.3 2.3 all_gather.11
  840.4 0.6 reshape.44
  841.2 0.6 reshape.45
  841.9 1.8 constant_dynamic-update-slice_fusion.2
  843.8 2.0 constant_dynamic-update-slice_fusion.1
  845.8 2.0 constant_dynamic-update-slice_fusion
  847.9 3.6 fusion.45
  851.5 5.9 copy.44
  857.4 6.0 copy.45
  863.3 34.7 %while.11 = (s32[]{:T(128)}, bf16[5,448,128]{2,1,0:T(8,128)(2,1)S(1)}, bf16[5,448,128]{2,1,0:T(8,128)(2,1)S(1)}, bf16[5,2688,128]{1,2,0:T(8,128)(2,1)}, bf16[5,2...) while((s32[]{:T(128)}, ...), condition=%wide.region_7.8_spmd.clone, body=%wide.region_2.7_spmd.clone.sunk | while | flops 747133696 | bytes 19685108 | solution.py:74
  863.4 2.1 fusion.66
  865.6 1.0 fusion.67
  866.5 2.0 fusion.68
  868.5 0.7 iota_compare_fusion.3
  869.2 0.4 fusion.69
  869.6 0.3 fusion.70
  869.9 0.4 fusion.71
  870.4 2.1 fusion.66
  872.5 1.0 fusion.67
  873.5 2.0 fusion.68
  875.5 0.7 iota_compare_fusion.3
  876.1 0.4 fusion.69
  876.8 0.4 fusion.71
  877.3 2.1 fusion.66
  879.4 1.0 fusion.67
  880.4 2.0 fusion.68
  882.4 0.7 iota_compare_fusion.3
  883.1 0.4 fusion.69
  883.8 0.4 fusion.71
  884.3 2.1 fusion.66
  886.4 1.0 fusion.67
  887.4 2.0 fusion.68
  889.4 0.7 iota_compare_fusion.3
  890.0 0.4 fusion.69
  890.7 0.4 fusion.71
  891.2 2.1 fusion.66
  893.3 1.0 fusion.67
  894.3 2.0 fusion.68
  896.3 0.7 iota_compare_fusion.3
  897.0 0.4 fusion.69
  897.6 0.4 fusion.71
  898.1 0.8 copy-done.4
  898.9 1.5 copy.55
  900.3 0.7 all_to_all.72
  901.0 87.7 %all_to_all.81 = bf16[8,56,640]{2,1,0:T(8,128)(2,1)S(1)} all-to-all(bf16[8,56,640]{2,1,0:T(8,128)(2,1)S(1)} %all_to_all.72), channel_id=1, replica_groups=mesh['head'=8,'blk'=32,'enc'=2] {'head'}, dimensions={0} | all-to-all | bytes 1146880 | tf_op jit(solution)/shard_map/all_to_all | solution.py:86
  988.8 1.1 broadcast_in_dim.59
  (43 shorter events, 3.2 us)
Async XLA Ops:
  6.5 305.0 %copy-start = (bf16[128,640]{1,0:T(8,128)(2,1)S(1)}, bf16[128,640]{1,0:T(8,128)(2,1)}, u32[]{:S(2)}) copy-start(bf16[128,640]{1,0:T(8,128)(2,1)} %param.16) | copy-start | bytes 491524
  7.7 102.9 %copy-start.1 = (bf16[1,56,5120]{2,1,0:T(8,128)(2,1)S(1)}, bf16[1,56,5120]{2,1,0:T(8,128)(2,1)}, u32[]{:S(2)}) copy-start(bf16[1,56,5120]{2,1,0:T(8,128)(2,1)} %param.11) | copy-start | bytes 1720324
  8.6 35.3 %all-to-all-start.1 = ((bf16[56,8,640]{2,0,1:T(8,128)(2,1)}), bf16[56,8,640]{2,0,1:T(8,128)(2,1)S(1)}, u32[]{:S(2)}, u32[]{:S(2)}) async-start(bf16[56,8,640]{2,0,1:T(8,128)(2,1)} %copy.42), calls=%async_computation.1 | async-start | bytes 1146880 | tf_op jit(solution)/shard_map/all_to_all | solution.py:45
  21.7 86.8 %all-gather.2.cloned.1.call-start = ((), (), s32[]{:S(2)}) async-start(), calls=%async_computation.5 | async-start | bytes 3440640 | tf_op jit(solution)/shard_map/all_gather | solution.py:57
  22.8 98.4 %copy-start.2 = (bf16[1,56,5120]{2,1,0:T(8,128)(2,1)S(1)}, bf16[1,56,5120]{2,1,0:T(8,128)(2,1)}, u32[]{:S(2)}) copy-start(bf16[1,56,5120]{2,1,0:T(8,128)(2,1)} %param.14) | copy-start | bytes 1720324
  85.2 226.3 %copy-start.5 = (bf16[256,128]{1,0:T(8,128)(2,1)S(1)}, bf16[256,128]{1,0:T(8,128)(2,1)}, u32[]{:S(2)}) copy-start(bf16[256,128]{1,0:T(8,128)(2,1)} %param.15) | copy-start | bytes 196612
  86.4 225.4 %copy-start.6 = (bf16[128,640]{1,0:T(8,128)(2,1)S(1)}, bf16[128,640]{1,0:T(8,128)(2,1)}, u32[]{:S(2)}) copy-start(bf16[128,640]{1,0:T(8,128)(2,1)} %param.17) | copy-start | bytes 491524
  108.4 201.1 %collective-permute-start = (bf16[2,896,640]{2,1,0:T(8,128)(2,1)}, bf16[2,896,640]{2,1,0:T(8,128)(2,1)}, u32[]{:S(2)}, u32[]{:S(2)}) collective-permute-start(bf16[2,896,640]{2,1,0:T(8,128)(2,1)} %all-gather.2.cloned.1.call-done), channel_id=1, source_target_pairs={{0,2},{2,4},{4,6},{6,8},{8,10},{10,12},{12,14},{14,16},{16,18},{18... | collective-permute-start | bytes 6881288 | tf_op jit(solution)/shard_map/ppermute | solution.py:13
  111.5 32.5 %all-to-all-start = ((bf16[56,8,640]{2,0,1:T(8,128)(2,1)}), bf16[56,8,640]{2,0,1:T(8,128)(2,1)S(1)}, u32[]{:S(2)}, u32[]{:S(2)}) async-start(bf16[56,8,640]{2,0,1:T(8,128)(2,1)} %copy.41), calls=%async_computation | async-start | bytes 1146880 | tf_op jit(solution)/shard_map/all_to_all | solution.py:44
  144.0 697.1 %all-to-all-start.3 = ((bf16[56,8,640]{2,0,1:T(8,128)(2,1)}), bf16[56,8,640]{2,0,1:T(8,128)(2,1)S(1)}, u32[]{:S(2)}, u32[]{:S(2)}) async-start(bf16[56,8,640]{2,0,1:T(8,128)(2,1)} %copy.46), calls=%async_computation.3 | async-start | bytes 1146880 | tf_op jit(solution)/shard_map/all_to_all | solution.py:47
  309.6 536.2 %collective-permute-start.1 = (bf16[2,896,640]{2,1,0:T(8,128)(2,1)}, bf16[2,896,640]{2,1,0:T(8,128)(2,1)}, u32[]{:S(2)}, u32[]{:S(2)}) collective-permute-start(bf16[2,896,640]{2,1,0:T(8,128)(2,1)} %collective-permute-done), channel_id=1, source_target_pairs={{0,2},{2,4},{4,6},{6,8},{8,10},{10,12},{12,14},{14,16},{16,18},{18... | collective-permute-start | bytes 6881288 | tf_op jit(solution)/shard_map/ppermute | solution.py:13
  857.4 6.0 copy-start.3
  898.1 0.8 copy-start.4
Sparse Core Ops, SparseCore 0:
  86.5 21.8 all-gather.1
where the time goes:
time: 998 us; the launch traced here: 997 us
  blocking collectives  656 us (66%)
  waiting for transfers between devices  218 us (22%)
  starting transfers between devices  39.1 us (4%)
  local copies, waits for them, and re-layouts  33 us (3%)
  matrix products  24.8 us (2%)
  between operations  14.3 us (1%)
  other arithmetic  10.9 us (1%)
    psum x1, blocking collectives, body(): key_total, value_total = lax.psum((key_part, value_part), 'blk')  509 us
    ppermute x2, waiting for transfers between devices, passed_along(): return lax.ppermute(value, axis, pairs)  153 us
    all_to_all x1, blocking collectives, body(): lax.all_to_all(token_major, 'head', split_axis=0, concat_axis=1, tiled=True)  87.7 us
    all_to_all x1, blocking collectives, body(): lax.all_to_all(value_rows[0], 'head', split_axis=1, concat_axis=0, tiled=...  41.4 us
    all_gather x1, waiting for transfers between devices, body(): source = lax.all_gather(stacked, 'enc', axis=1, tiled=True)  22 us
    all_to_all x1, waiting for transfers between devices, body(): lax.all_to_all(queries[0], 'head', split_axis=1, concat_axis=0, tiled=True)  21.9 us
    all_to_all x1, waiting for transfers between devices, body(): lax.all_to_all(key_rows[0], 'head', split_axis=1, concat_axis=0, tiled=True)  21 us
  transfers between devices with their start and end apart: 6, of which 4 were waited for; matrix products, arithmetic and copies ran while one was open for 1% of the time, Pallas kernels for 0%

commit v1 on v0

v1 whole, which is shorter than its diff:
```python
import functools

import jax
import jax.numpy as jnp
from jax import lax
from jax.experimental import pallas as pl
from jax.experimental.pallas import tpu as pltpu
from jax.sharding import PartitionSpec as P

HEAD_DIM = 128
STOPS = 3
MESH = pl.DeviceIdType.MESH
COLUMNS = 16
RING = 16
SOURCES = 16
SLOTS = 3
SCORE = float(HEAD_DIM) ** -0.5 * 1.4426950408889634
OUT = 1.0e30


def kernel(
    q_ref, k_ref, v_ref, tq_ref, emb_ref, wk_ref, wv_ref, stop_ref, plen_ref, out_ref,
    kv_in, q_in, kv, part, part_in, total, other, text, result, stops,
    kv_recv, q_recv, send, fwd_send, fwd_recv, o_send, o_recv, t_send, t_recv,
):
    g = lax.axis_index("head")
    b = lax.axis_index("blk")
    e = lax.axis_index("enc")
    p = b // COLUMNS
    c = b % COLUMNS
    z = p * 8 + g
    wide = p == g % 2
    home = e == p
    my_col = g * 640 + jnp.where(wide, 0, 384)
    slot = g * 2 + e
    tokens = kv_in.shape[3]
    rows = SOURCES * tokens

    barrier = pltpu.get_barrier_semaphore()

    def greet(device):
        pl.semaphore_signal(barrier, inc=1, device_id=device, device_id_type=MESH)

    def greet_z(n, _):
        tg, tp = n % 8, n // 8

        @pl.when(jnp.logical_or(n != z, jnp.logical_not(home)))
        def _():
            greet((tg, tp * COLUMNS + c, p))

        return 0

    def greet_givers(n, _):
        greet((n, e * COLUMNS + c, 1 - p))
        return 0

    def greet_plane(n, _):
        greet((g, p * COLUMNS + (c + n // 2) % COLUMNS, n % 2))
        return 0

    lax.fori_loop(0, RING, greet_z, 0)
    lax.fori_loop(0, 8, greet_givers, 0)
    lax.fori_loop(2, 2 * COLUMNS, greet_plane, 0)

    @pl.when(home)
    def _():
        pl.semaphore_wait(barrier, 53)

    @pl.when(jnp.logical_not(home))
    def _():
        pl.semaphore_wait(barrier, 54)

    def send_heads(hs, refs, landing, recv, sends):
        def one(n, _):
            m = RING - 1 - n
            t = (z + ((m + 1) // 2) * (2 * (m % 2) - 1) + RING) % RING
            tg, tp = t % 8, t // 8
            t_wide = tp == tg % 2
            col = pl.multiple_of(tg * 640 + jnp.where(t_wide, 0, 384) + hs * HEAD_DIM, HEAD_DIM)
            mine = jnp.logical_and(t == z, home)
            needed = t_wide if hs == 2 else True

            @pl.when(jnp.logical_and(jnp.logical_not(mine), needed))
            def _():
                for i, ref in enumerate(refs):
                    pltpu.make_async_remote_copy(
                        src_ref=ref.at[:, pl.ds(col, HEAD_DIM)],
                        dst_ref=landing.at[hs, i, slot],
                        send_sem=send.at[sends + i],
                        recv_sem=recv.at[hs],
                        device_id=(tg, tp * COLUMNS + c, p),
                        device_id_type=MESH,
                    ).start()

            @pl.when(jnp.logical_and(mine, needed))
            def _():
                for i, ref in enumerate(refs):
                    pltpu.make_async_copy(
                        ref.at[:, pl.ds(col, HEAD_DIM)], landing.at[hs, i, slot], recv.at[hs]
                    ).start()

            return 0

        lax.fori_loop(0, RING, one, 0)

    def wait_for(ref, sem):
        pltpu.make_async_copy(ref, ref, sem).wait()

    def per_slot(hs, run):
        if hs == 2:
            pl.when(wide)(run)
        else:
            run()

    def forward(hs, m):
        next_c = (c + 1) % COLUMNS
        next_e = jnp.where(c == COLUMNS - 1, 1 - e, e)
        return pltpu.make_async_remote_copy(
            src_ref=kv.at[m, hs],
            dst_ref=kv.at[m + 1, hs],
            send_sem=fwd_send.at[m, hs],
            recv_sem=fwd_recv.at[m, hs],
            device_id=(g, p * COLUMNS + next_c, next_e),
            device_id_type=MESH,
        )

    def keys_arrive(hs):
        def run():
            wait_for(kv_in.at[hs], kv_recv.at[hs])
            for i in range(2):
                whole = kv_in[hs, i].astype(jnp.float32).reshape(rows, HEAD_DIM)
                kv[0, hs, i] = whole.astype(jnp.bfloat16)
            forward(hs, 0).start()

        per_slot(hs, run)

    def keys_pass(hs):
        def run():
            forward(hs, 0).wait_recv()
            forward(hs, 1).start()

        per_slot(hs, run)

    send_heads(0, (k_ref, v_ref), kv_in, kv_recv, 0)

    stops[0] = jnp.full((8, 128), stop_ref[0].astype(jnp.float32))
    trade = pltpu.make_async_remote_copy(
        src_ref=stops.at[0],
        dst_ref=stops.at[1],
        send_sem=t_send.at[3],
        recv_sem=t_recv.at[3],
        device_id=(g, (1 - p) * COLUMNS + c, e),
        device_id_type=MESH,
    )
    trade.start()

    for i, w_ref in enumerate((wk_ref, wv_ref)):
        product = jnp.dot(emb_ref[...], w_ref[...], preferred_element_type=jnp.float32)
        part[:, i] = product.reshape(part.shape[0], part.shape[2], part.shape[3])

    def send_part(n, _):
        cc = (c + n) % COLUMNS
        pltpu.make_async_remote_copy(
            src_ref=part.at[cc],
            dst_ref=part_in.at[c],
            send_sem=t_send.at[0],
            recv_sem=t_recv.at[0],
            device_id=(g, p * COLUMNS + cc, e),
            device_id_type=MESH,
        ).start()
        return 0

    lax.fori_loop(1, COLUMNS, send_part, 0)
    part_in[c] = part[c]

    send_heads(1, (k_ref, v_ref), kv_in, kv_recv, 0)
    keys_arrive(0)
    send_heads(2, (k_ref, v_ref), kv_in, kv_recv, 0)

    wait_for(part_in.at[pl.ds(0, COLUMNS - 1)], t_recv.at[0])
    total[...] = jnp.sum(part_in[...], axis=0)

    def swap(left):
        cols = (384, 256) if left else (0, 384)
        return pltpu.make_async_remote_copy(
            src_ref=total.at[:, :, pl.ds(*cols)],
            dst_ref=other.at[:, :, pl.ds(0, cols[1])],
            send_sem=t_send.at[1],
            recv_sem=t_recv.at[1],
            device_id=(g, (1 - p) * COLUMNS + c, e),
            device_id_type=MESH,
        )

    @pl.when(wide)
    def _():
        swap(True).start()

    @pl.when(jnp.logical_not(wide))
    def _():
        swap(False).start()

    keys_arrive(1)
    send_heads(0, (q_ref, tq_ref), q_in, q_recv, 2)
    keys_pass(0)

    chunk = e * COLUMNS + c

    @pl.when(wide)
    def _():
        swap(False).wait_recv()
        text[chunk] = (total[:, :, 0:384] + other[...]).astype(jnp.bfloat16)

    @pl.when(jnp.logical_not(wide))
    def _():
        swap(True).wait_recv()
        both = (total[:, :, 384:640] + other[:, :, 0:256]).astype(jnp.bfloat16)
        text[chunk, :, :, 0:256] = both
        text[chunk, :, :, 256:384] = jnp.zeros((2, 16, 128), jnp.bfloat16)

    def send_text(n, _):
        pltpu.make_async_remote_copy(
            src_ref=text.at[chunk],
            dst_ref=text.at[chunk],
            send_sem=t_send.at[2],
            recv_sem=t_recv.at[2],
            device_id=(g, p * COLUMNS + (c + n // 2) % COLUMNS, (e + n) % 2),
            device_id_type=MESH,
        ).start()
        return 0

    lax.fori_loop(1, 2 * COLUMNS, send_text, 0)

    keys_arrive(2)
    send_heads(1, (q_ref, tq_ref), q_in, q_recv, 2)
    keys_pass(1)
    send_heads(2, (q_ref, tq_ref), q_in, q_recv, 2)
    keys_pass(2)
    wait_for(text.at[pl.ds(0, 2 * COLUMNS - 1)], t_recv.at[2])

    group = 4
    trade.wait()
    here = jnp.where(home, 1.0, 0.0)
    stop = stops[0, 0:1, 0:1] * here + stops[1, 0:1, 0:1] * (1.0 - here)
    shut = [jnp.where(m < stop, 0.0, OUT) for m in range(STOPS)]
    live = lax.broadcasted_iota(jnp.int32, (1, 2 * COLUMNS * 16), 1) < plen_ref[0]

    def attend(hs):
        def block(i, _):
            query, cross = (
                q_in[hs, j, pl.ds(i * group, group)].astype(jnp.float32).reshape(group * tokens, HEAD_DIM).astype(jnp.bfloat16)
                for j in range(2)
            )
            scores = [
                lax.dot_general(query, kv[m, hs, 0], (((1,), (1,)), ((), ())), preferred_element_type=jnp.float32)
                for m in range(STOPS)
            ]
            peaks = [jnp.max(s, axis=1, keepdims=True) - shut[m] for m, s in enumerate(scores)]
            peak = jnp.maximum(jnp.maximum(peaks[0], peaks[1]), peaks[2]) * SCORE
            weights = [jnp.exp2(s * SCORE - (peak + shut[m])) for m, s in enumerate(scores)]
            sums = sum(jnp.sum(w, axis=1, keepdims=True) for w in weights)
            mix = sum(
                jnp.dot(w.astype(jnp.bfloat16), kv[m, hs, 1], preferred_element_type=jnp.float32)
                for m, w in enumerate(weights)
            )
            text_keys = text[:, 0, :, hs * 128 : hs * 128 + 128].reshape(512, HEAD_DIM)
            text_values = text[:, 1, :, hs * 128 : hs * 128 + 128].reshape(512, HEAD_DIM)
            scores = lax.dot_general(cross, text_keys, (((1,), (1,)), ((), ())), preferred_element_type=jnp.float32)
            scores = jnp.where(live, scores, -OUT)
            weights = jnp.exp2((scores - jnp.max(scores, axis=1, keepdims=True)) * SCORE)
            cross_mix = jnp.dot(weights.astype(jnp.bfloat16), text_values, preferred_element_type=jnp.float32)
            mixed = mix / sums + cross_mix / jnp.sum(weights, axis=1, keepdims=True)
            result[hs, pl.ds(i * group, group)] = mixed.reshape(group, tokens, HEAD_DIM).astype(jnp.bfloat16)

            def give(n, _):
                s = i * group + n
                mine = jnp.logical_and(s == slot, home)
                where = out_ref.at[:, pl.ds(pl.multiple_of(my_col + hs * HEAD_DIM, HEAD_DIM), HEAD_DIM)]

                @pl.when(jnp.logical_not(mine))
                def _():
                    pltpu.make_async_remote_copy(
                        src_ref=result.at[hs, s],
                        dst_ref=where,
                        send_sem=o_send.at[hs],
                        recv_sem=o_recv,
                        device_id=(s // 2, e * COLUMNS + c, s % 2),
                        device_id_type=MESH,
                    ).start()

                @pl.when(mine)
                def _():
                    pltpu.make_async_copy(result.at[hs, s], where, o_recv).start()

                return 0

            lax.fori_loop(0, group, give, 0)
            return 0

        def run():
            wait_for(q_in.at[hs], q_recv.at[hs])
            forward(hs, 1).wait_recv()
            lax.fori_loop(0, SOURCES // group, block, 0)

        per_slot(hs, run)

    for hs in range(SLOTS):
        attend(hs)

    def token_sends(width):
        for i, ref in enumerate((k_ref, v_ref, q_ref, tq_ref)):
            wait_for(ref.at[:, pl.ds(0, width * HEAD_DIM)], send.at[i])

    @pl.when(jnp.logical_not(home))
    def _():
        token_sends(40)

    @pl.when(jnp.logical_and(home, wide))
    def _():
        token_sends(37)

    @pl.when(jnp.logical_and(home, jnp.logical_not(wide)))
    def _():
        token_sends(38)

    wait_for(part.at[pl.ds(0, COLUMNS - 1)], t_send.at[0])

    @pl.when(wide)
    def _():
        swap(True).wait_send()

    @pl.when(jnp.logical_not(wide))
    def _():
        swap(False).wait_send()

    wait_for(text.at[pl.ds(0, 2 * COLUMNS - 1)], t_send.at[2])
    for hs in range(SLOTS):

        def finish(hs=hs):
            forward(hs, 0).wait_send()
            forward(hs, 1).wait_send()

            @pl.when(home)
            def _():
                wait_for(result.at[hs, pl.ds(0, SOURCES - 1)], o_send.at[hs])

            @pl.when(jnp.logical_not(home))
            def _():
                wait_for(result.at[hs], o_send.at[hs])

        per_slot(hs, finish)
    wait_for(out_ref, o_recv)


def body(
    queries,
    key_rows,
    value_rows,
    text_queries,
    prompt_embed,
    key_weight,
    value_weight,
    stop_count,
    prompt_length,
):
    tokens, width = queries.shape[1:]
    heads_here = key_weight.shape[1]
    text_rows = prompt_embed.shape[0] // COLUMNS
    dma = pltpu.SemaphoreType.DMA
    mixed = pl.pallas_call(
        kernel,
        out_shape=jax.ShapeDtypeStruct((tokens, width), jnp.bfloat16),
        in_specs=[pl.BlockSpec(memory_space=pl.ANY)] * 4
        + [pl.BlockSpec(memory_space=pltpu.VMEM)] * 3
        + [pl.BlockSpec(memory_space=pltpu.SMEM)] * 2,
        out_specs=pl.BlockSpec(memory_space=pl.ANY),
        scratch_shapes=[
            pltpu.VMEM((SLOTS, 2, SOURCES, tokens, HEAD_DIM), jnp.bfloat16),
            pltpu.VMEM((SLOTS, 2, SOURCES, tokens, HEAD_DIM), jnp.bfloat16),
            pltpu.VMEM((STOPS, SLOTS, 2, SOURCES * tokens, HEAD_DIM), jnp.bfloat16),
            pltpu.VMEM((COLUMNS, 2, text_rows, heads_here), jnp.float32),
            pltpu.VMEM((COLUMNS, 2, text_rows, heads_here), jnp.float32),
            pltpu.VMEM((2, text_rows, heads_here), jnp.float32),
            pltpu.VMEM((2, text_rows, SLOTS * HEAD_DIM), jnp.float32),
            pltpu.VMEM((2 * COLUMNS, 2, text_rows, SLOTS * HEAD_DIM), jnp.bfloat16),
            pltpu.VMEM((SLOTS, SOURCES, tokens, HEAD_DIM), jnp.bfloat16),
            pltpu.VMEM((2, 8, 128), jnp.float32),
            dma((SLOTS,)),
            dma((SLOTS,)),
            dma((4,)),
            dma((2, SLOTS)),
            dma((2, SLOTS)),
            dma((SLOTS,)),
            dma,
            dma((4,)),
            dma((4,)),
        ],
        compiler_params=pltpu.CompilerParams(
            collective_id=0, has_side_effects=True, vmem_limit_bytes=48 * 1024 * 1024
        ),
    )(
        queries[0],
        key_rows[0],
        value_rows[0],
        text_queries[0],
        prompt_embed,
        key_weight,
        value_weight,
        stop_count,
        prompt_length,
    )
    return mixed[None]


def solution(mesh):
    placed = (
        P("blk", ("head", "enc"), None),
        P("blk", ("head", "enc"), None),
        P("blk", ("head", "enc"), None),
        P("blk", ("head", "enc"), None),
        P("enc", "blk"),
        P("blk", "head"),
        P("blk", "head"),
        P("blk"),
        P(),
    )
    return jax.shard_map(
        body, mesh=mesh, in_specs=placed, out_specs=P("blk", ("head", "enc"), None), check_vma=False
    )
```

time: 998 us -> 163 us (0.16)
  blocking collectives: 656 us -> 0 us
  waiting for transfers between devices: 218 us -> 0 us
  Pallas kernels: 0 us -> 153 us
  starting transfers between devices: 39.1 us -> 0 us
  local copies, waits for them, and re-layouts: 33 us -> 7.71 us
  matrix products: 24.8 us -> 0 us
  between operations: 14.3 us -> 1.32 us
  other arithmetic: 10.9 us -> 0 us
    psum x1 -> x0, blocking collectives: 509 us -> none  [body(): key_total, value_total = lax.psum((key_part, value_part), 'blk')]
    pallas_call x0 -> x1, Pallas kernels: none -> 153 us  [body(): pl.pallas_call(kernel, out_shape=jax.ShapeDtypeStruct((tokens, width), jn...]
    ppermute x2 -> x0, waiting for transfers between devices: 153 us -> none  [passed_along(): return lax.ppermute(value, axis, pairs)]
    all_to_all x2 -> x0, blocking collectives: 129 us -> none  [the longest x1 87.7 us: body(): lax.all_to_all(token_major, 'head', split_axis=0, concat_axis=1, tiled=True)]
    all_to_all x3 -> x0, waiting for transfers between devices: 42.8 us -> none  [the longest x1 21.9 us: body(): lax.all_to_all(queries[0], 'head', split_axis=1, concat_axis=0, tiled=True)]
    all_to_all x3 -> x0, starting transfers between devices: 35.1 us -> none  [the longest x1 13.1 us: body(): lax.all_to_all(key_rows[0], 'head', split_axis=1, concat_axis=0, tiled=True)]
    dot_general x22 -> x0, matrix products: 24.8 us -> none  [the longest x10 12.5 us: head_attention(): jnp.einsum('qd,kd->qk', head_query, known_keys, preferred_element_type=jn...]
    all_gather x1 -> x0, waiting for transfers between devices: 22 us -> none  [body(): source = lax.all_gather(stacked, 'enc', axis=1, tiled=True)]
  transfers between devices with their start and end apart: 6 -> 0, of which waited for: 4 -> 0; matrix products, arithmetic and copies ran while one was open for 1% -> 0% of each run, Pallas kernels for 0% -> 0%
where the time goes in v1:
time: 163 us
  Pallas kernels  153 us (94%)
  local copies, waits for them, and re-layouts  7.71 us (5%)
    pallas_call x1, Pallas kernels, body(): pl.pallas_call(kernel, out_shape=jax.ShapeDtypeStruct((tokens, width), jn...  153 us
    unnamed x15, local copies, waits for them, and re-layouts  7.71 us

profile of v1, /device:TPU:1, one launch (start us, length us, event | category | flops | bytes accessed | tf_op | source)
XLA Modules:
  0.0 162.5 jit_solution(8522153760211545897)
XLA Ops:
  1.3 0.0 copy-start
  1.3 1.1 copy-done
  2.4 0.0 copy-start.1
  2.4 1.1 copy-done.1
  3.4 0.0 copy-start.2
  3.4 1.1 copy-done.2
  4.5 0.0 copy-start.3
  4.5 1.1 copy-done.3
  5.5 0.0 copy-start.4
  5.5 0.9 copy-done.4
  6.5 0.0 copy-start.5
  6.5 0.9 copy-done.5
  7.4 0.0 copy-start.6
  7.4 0.8 copy-done.6
  8.2 153.5 %shard_map.91 = bf16[56,5120]{1,0:T(8,128)(2,1)S(1)} custom-call(bf16[56,5120]{1,0:T(8,128)(2,1)S(1)} %bitcast.6, bf16[56,5120]{1,0:T(8,128)(2,1)S(1)} %bitcast.7, bf16[56,5120]{1,0:T(8,128)(2,1)S(1)} %bitcast.8, bf16[56,5120]{1,0:T(8,128)(2,1)S(1)} %bitcast.9, bf16[256,128]{1,0:T(8,128)(2,1)S(1)} %copy-done.6, bf16[128,640]{1,0:T(8,128)(2,1)S(1)} %copy-done.4, ...), custom_call_target="tpu_custom_call" | custom-call | tf_op jit(solution)/shard_map/pallas_call | solution.py:369
  161.7 0.8 copy.13
Async XLA Ops:
  1.3 1.1 copy-start
  2.4 1.1 copy-start.1
  3.4 1.1 copy-start.2
  4.5 1.1 copy-start.3
  5.5 0.9 copy-start.4
  6.5 0.9 copy-start.5
  7.4 0.8 copy-start.6

commit v2 on v1

v2 whole, which is shorter than its diff:
```python
import functools

import jax
import jax.numpy as jnp
from jax import lax
from jax.experimental import pallas as pl
from jax.experimental.pallas import tpu as pltpu
from jax.sharding import PartitionSpec as P

HEAD_DIM = 128
STOPS = 3
MESH = pl.DeviceIdType.MESH
COLUMNS = 16
RING = 16
SOURCES = 16
SLOTS = 3
SCORE = float(HEAD_DIM) ** -0.5 * 1.4426950408889634
OUT = 1.0e30
TRADE, PART, SWAP, ASK, UP, ROWS, ANSWER = range(7)


def kernel(
    q_ref, k_ref, v_ref, tq_ref, emb_hbm, wk_hbm, wv_hbm, stop_ref, plen_ref, out_ref,
    kv_in, q_in, kv, part, part_in, total, other, piece, column, text, result, stops, emb_ref, wk_ref, wv_ref,
    cross_in, cross_out, self_mix, cross_mix,
    kv_recv, q_recv, send, fwd_send, fwd_recv, o_send, o_recv, t_send, t_recv, w_sem,
):
    g = lax.axis_index("head")
    b = lax.axis_index("blk")
    e = lax.axis_index("enc")
    p = b // COLUMNS
    c = b % COLUMNS
    x, y = c // 4, c % 4
    z = p * 8 + g
    wide = z % 2 == 0
    home = e == p
    my_col = (z // 2) * 640 + jnp.where(wide, 0, 384)
    slot = g * 2 + e
    tokens = kv_in.shape[3]
    rows = SOURCES * tokens

    weights = [
        pltpu.make_async_copy(source, place, w_sem.at[i])
        for i, (source, place) in enumerate(((emb_hbm, emb_ref), (wk_hbm, wk_ref), (wv_hbm, wv_ref)))
    ]
    for copy in weights:
        copy.start()

    barrier = pltpu.get_barrier_semaphore()

    def greet(device):
        pl.semaphore_signal(barrier, inc=1, device_id=device, device_id_type=MESH)

    def at(height, core):
        return (height % 8, (height // 8) * COLUMNS + c, core)

    def beside(where, core):
        return (g, p * COLUMNS + where, core)

    def greet_column(n, _):
        height, core = n // 2, n % 2

        @pl.when(jnp.logical_or(height != z, core != e))
        def _():
            greet(at(height, core))

        return 0

    def greet_plane(n, _):
        greet(beside((c + n // 2) % COLUMNS, n % 2))
        return 0

    lax.fori_loop(0, 2 * RING, greet_column, 0)
    lax.fori_loop(2, 2 * COLUMNS, greet_plane, 0)
    pl.semaphore_wait(barrier, 61)

    def copy_to(source, place, kind, device):
        return pltpu.make_async_remote_copy(
            src_ref=source,
            dst_ref=place,
            send_sem=t_send.at[kind],
            recv_sem=t_recv.at[kind],
            device_id=device,
            device_id_type=MESH,
        )

    def give(mine, source, place, kind, device):
        @pl.when(jnp.logical_not(mine))
        def _():
            copy_to(source, place, kind, device).start()

        @pl.when(mine)
        def _():
            pltpu.make_async_copy(source, place, t_recv.at[kind]).start()

    def send_heads(kind, hs, half):
        refs, landing, recv = ((k_ref, v_ref), kv_in, kv_recv) if kind == 0 else ((q_ref,), q_in, q_recv)

        def one(n, _):
            m = jnp.where(n % 2 == 0, RING - 1 - n // 2, n // 2)
            t = (z + ((m + 1) // 2) * (2 * (m % 2) - 1) + RING) % RING
            col = pl.multiple_of((t // 2) * 640 + (t % 2) * 384 + hs * HEAD_DIM, HEAD_DIM)
            mine = jnp.logical_and(t == z, home)
            needed = t % 2 == 0 if hs == 2 else True

            @pl.when(jnp.logical_and(jnp.logical_not(mine), needed))
            def _():
                for i, ref in enumerate(refs):
                    pltpu.make_async_remote_copy(
                        src_ref=ref.at[:, pl.ds(col, HEAD_DIM)],
                        dst_ref=landing.at[hs, i, slot],
                        send_sem=send.at[kind, hs, half],
                        recv_sem=recv.at[hs],
                        device_id=at(t, p),
                        device_id_type=MESH,
                    ).start()

            @pl.when(jnp.logical_and(mine, needed))
            def _():
                for i, ref in enumerate(refs):
                    pltpu.make_async_copy(
                        ref.at[:, pl.ds(col, HEAD_DIM)], landing.at[hs, i, slot], recv.at[hs]
                    ).start()

            return 0

        lax.fori_loop(8 * half, 8 * half + 8, one, 0)

    def sent(kind, hs, half):
        landing = kv_in if kind == 0 else q_in
        count = 4 if hs == 2 else 8

        def left(copies):
            wait_for(landing.at[hs, :, pl.ds(0, copies)], send.at[kind, hs, half])

        if half == 1:
            left(count)
            return
        keeps = jnp.logical_and(home, wide) if hs == 2 else home

        @pl.when(keeps)
        def _():
            left(count - 1)

        @pl.when(jnp.logical_not(keeps))
        def _():
            left(count)

    def wait_for(ref, sem):
        pltpu.make_async_copy(ref, ref, sem).wait()

    def per_slot(hs, run):
        if hs == 2:
            pl.when(wide)(run)
        else:
            run()

    def forward(hs, m):
        next_c = (c + 1) % COLUMNS
        next_e = jnp.where(c == COLUMNS - 1, 1 - e, e)
        return pltpu.make_async_remote_copy(
            src_ref=kv.at[m, hs],
            dst_ref=kv.at[m + 1, hs],
            send_sem=fwd_send.at[m, hs],
            recv_sem=fwd_recv.at[m, hs],
            device_id=(g, p * COLUMNS + next_c, next_e),
            device_id_type=MESH,
        )

    def keys_arrive(hs):
        def run():
            wait_for(kv_in.at[hs], kv_recv.at[hs])
            for i in range(2):
                whole = kv_in[hs, i].astype(jnp.float32).reshape(rows, HEAD_DIM)
                kv[0, hs, i] = whole.astype(jnp.bfloat16)
            forward(hs, 0).start()

        per_slot(hs, run)

    def keys_pass(hs):
        def run():
            forward(hs, 0).wait_recv()
            forward(hs, 1).start()

        per_slot(hs, run)


    send_heads(0, 0, 0)
    send_heads(0, 0, 1)

    stops[0] = jnp.full((8, 128), stop_ref[0].astype(jnp.float32))
    trade = copy_to(stops.at[0], stops.at[1], TRADE, at((1 - p) * 8 + g, e))
    trade.start()

    for copy in weights:
        copy.wait()

    for i, w_ref in enumerate((wk_ref, wv_ref)):
        product = jnp.dot(emb_ref[...], w_ref[...], preferred_element_type=jnp.float32)
        part[:, i] = product.reshape(part.shape[0], part.shape[2], part.shape[3])

    def send_part(n, _):
        cc = (c + n) % COLUMNS
        copy_to(part.at[cc], part_in.at[c], PART, beside(cc, e)).start()
        return 0

    lax.fori_loop(1, COLUMNS, send_part, 0)
    part_in[c] = part[c]

    lot = 5 * HEAD_DIM
    mine5 = 2 * x + e

    def send_cross(n, _):
        to = (mine5 + n) % 8
        source = tq_ref.at[:, pl.ds(pl.multiple_of(to * lot, HEAD_DIM), lot)]
        give(n == 0, source, cross_in.at[mine5], ASK, beside((to // 2) * 4 + y, to % 2))
        return 0

    lax.fori_loop(0, 8, send_cross, 0)

    sent(0, 0, 0)
    send_heads(0, 1, 0)
    sent(0, 0, 1)
    send_heads(0, 1, 1)
    keys_arrive(0)

    wait_for(part_in.at[pl.ds(0, COLUMNS - 1)], t_recv.at[PART])
    total[...] = jnp.sum(part_in[...], axis=0)
    for n in range(5):
        cols = pl.ds(n * HEAD_DIM, HEAD_DIM)
        copy_to(total.at[1 - p, :, cols], other.at[:, cols], SWAP, at((1 - p) * 8 + g, e)).start()

    sent(0, 1, 0)
    send_heads(0, 2, 0)
    send_heads(0, 2, 1)
    keys_pass(0)

    wait_for(other, t_recv.at[SWAP])
    piece[...] = (total[p] + other[...]).astype(jnp.bfloat16)
    column[p, g] = piece[...]

    def send_up(n, _):
        copy_to(piece, column.at[p, g], UP, at((z + n) % RING, e)).start()
        return 0

    lax.fori_loop(1, RING, send_up, 0)

    sent(0, 1, 1)
    send_heads(1, 0, 0)
    send_heads(1, 0, 1)
    keys_arrive(1)

    sent(0, 2, 0)
    sent(0, 2, 1)
    send_heads(1, 1, 0)
    send_heads(1, 1, 1)
    keys_arrive(2)
    keys_pass(1)

    sent(1, 0, 0)
    sent(1, 0, 1)
    send_heads(1, 2, 0)
    send_heads(1, 2, 1)
    keys_pass(2)

    group = 4
    trade.wait()
    here = jnp.where(home, 1.0, 0.0)
    stop = stops[0, 0:1, 0:1] * here + stops[1, 0:1, 0:1] * (1.0 - here)
    shut = [jnp.where(m < stop, 0.0, OUT) for m in range(STOPS)]
    at_row = lax.broadcasted_iota(jnp.int32, (1, 2 * COLUMNS * 16), 1)
    live = at_row < plen_ref[0]

    def flat(values):
        return values.astype(jnp.float32).reshape(-1, HEAD_DIM).astype(jnp.bfloat16)

    def cross():
        def head(h, _):
            cols = pl.ds(pl.multiple_of(h * HEAD_DIM, HEAD_DIM), HEAD_DIM)
            query = flat(cross_in[:, :, cols])
            text_keys = text[:, 0, :, cols].reshape(512, HEAD_DIM)
            text_values = text[:, 1, :, cols].reshape(512, HEAD_DIM)
            scores = lax.dot_general(query, text_keys, (((1,), (1,)), ((), ())), preferred_element_type=jnp.float32)
            scores = jnp.where(live, scores, -OUT)
            weights = jnp.exp2((scores - jnp.max(scores, axis=1, keepdims=True)) * SCORE)
            mix = jnp.dot(weights.astype(jnp.bfloat16), text_values, preferred_element_type=jnp.float32)
            mix = mix / jnp.sum(weights, axis=1, keepdims=True)
            cross_out[:, :, cols] = mix.reshape(8, tokens, HEAD_DIM).astype(jnp.bfloat16)
            return 0

        def answer(n, _):
            to = (mine5 + n) % 8
            place = cross_mix.at[:, pl.ds(pl.multiple_of(mine5 * lot, HEAD_DIM), lot)]
            give(n == 0, cross_out.at[to], place, ANSWER, beside((to // 2) * 4 + y, to % 2))
            return 0

        wait_for(cross_in, t_recv.at[ASK])
        wait_for(text, t_recv.at[ROWS])
        lax.fori_loop(0, 5, head, 0)
        lax.fori_loop(0, 8, answer, 0)

    def attend(hs):
        def block(i, _):
            query = flat(q_in[hs, 0, pl.ds(i * group, group)])
            scores = [
                lax.dot_general(query, kv[m, hs, 0], (((1,), (1,)), ((), ())), preferred_element_type=jnp.float32)
                for m in range(STOPS)
            ]
            peaks = [jnp.max(s, axis=1, keepdims=True) - shut[m] for m, s in enumerate(scores)]
            peak = jnp.maximum(jnp.maximum(peaks[0], peaks[1]), peaks[2]) * SCORE
            weights = [jnp.exp2(s * SCORE - (peak + shut[m])) for m, s in enumerate(scores)]
            sums = sum(jnp.sum(w, axis=1, keepdims=True) for w in weights)
            mix = sum(
                jnp.dot(w.astype(jnp.bfloat16), kv[m, hs, 1], preferred_element_type=jnp.float32)
                for m, w in enumerate(weights)
            )
            mixed = mix / sums
            result[hs, pl.ds(i * group, group)] = mixed.reshape(group, tokens, HEAD_DIM).astype(jnp.bfloat16)

            def hand_back(n, _):
                s = i * group + n
                mine = jnp.logical_and(s == slot, home)
                where = self_mix.at[:, pl.ds(pl.multiple_of(my_col + hs * HEAD_DIM, HEAD_DIM), HEAD_DIM)]

                @pl.when(jnp.logical_not(mine))
                def _():
                    pltpu.make_async_remote_copy(
                        src_ref=result.at[hs, s],
                        dst_ref=where,
                        send_sem=o_send.at[hs],
                        recv_sem=o_recv,
                        device_id=(s // 2, e * COLUMNS + c, s % 2),
                        device_id_type=MESH,
                    ).start()

                @pl.when(mine)
                def _():
                    pltpu.make_async_copy(result.at[hs, s], where, o_recv).start()

                return 0

            lax.fori_loop(0, group, hand_back, 0)
            return 0

        def run():
            wait_for(q_in.at[hs], q_recv.at[hs])
            forward(hs, 1).wait_recv()
            lax.fori_loop(0, SOURCES // group, block, 0)

        per_slot(hs, run)

    attend(0)

    wait_for(text.at[pl.ds(0, RING - 1), 0], t_recv.at[UP])
    chunk = e * COLUMNS + c

    def send_text(n, _):
        to, row = (mine5 + n // 4) % 8, (y + n) % 4
        give(n == 0, column.at[:, to], text.at[chunk], ROWS, beside((to // 2) * 4 + row, to % 2))
        return 0

    lax.fori_loop(0, 32, send_text, 0)

    attend(1)
    attend(2)
    cross()

    for hs in (1, 2):
        sent(1, hs, 0)
        sent(1, hs, 1)
    wait_for(part.at[pl.ds(0, COLUMNS - 1)], t_send.at[PART])
    wait_for(other, t_send.at[SWAP])
    wait_for(cross_in.at[pl.ds(0, 7)], t_send.at[ASK])
    wait_for(cross_out.at[pl.ds(0, 7)], t_send.at[ANSWER])
    wait_for(text.at[pl.ds(0, 31)], t_send.at[ROWS])
    wait_for(text.at[pl.ds(0, RING - 1), 0], t_send.at[UP])
    for hs in range(SLOTS):

        def finish(hs=hs):
            forward(hs, 0).wait_send()
            forward(hs, 1).wait_send()

            @pl.when(home)
            def _():
                wait_for(result.at[hs, pl.ds(0, SOURCES - 1)], o_send.at[hs])

            @pl.when(jnp.logical_not(home))
            def _():
                wait_for(result.at[hs], o_send.at[hs])

        per_slot(hs, finish)
    wait_for(cross_mix, t_recv.at[ANSWER])
    wait_for(self_mix, o_recv)
    out_ref[...] = (self_mix[...].astype(jnp.float32) + cross_mix[...].astype(jnp.float32)).astype(jnp.bfloat16)


def body(
    queries,
    key_rows,
    value_rows,
    text_queries,
    prompt_embed,
    key_weight,
    value_weight,
    stop_count,
    prompt_length,
):
    tokens, width = queries.shape[1:]
    heads_here = key_weight.shape[1]
    text_rows = prompt_embed.shape[0] // COLUMNS
    dma = pltpu.SemaphoreType.DMA
    mixed = pl.pallas_call(
        kernel,
        out_shape=jax.ShapeDtypeStruct((tokens, width), jnp.bfloat16),
        in_specs=[pl.BlockSpec(memory_space=pltpu.HBM)] * 7
        + [pl.BlockSpec(memory_space=pltpu.SMEM)] * 2,
        out_specs=pl.BlockSpec(memory_space=pltpu.VMEM),
        scratch_shapes=[
            pltpu.VMEM((SLOTS, 2, SOURCES, tokens, HEAD_DIM), jnp.bfloat16),
            pltpu.VMEM((SLOTS, 1, SOURCES, tokens, HEAD_DIM), jnp.bfloat16),
            pltpu.VMEM((STOPS, SLOTS, 2, SOURCES * tokens, HEAD_DIM), jnp.bfloat16),
            pltpu.VMEM((COLUMNS, 2, text_rows, heads_here), jnp.float32),
            pltpu.VMEM((COLUMNS, 2, text_rows, heads_here), jnp.float32),
            pltpu.VMEM((2, text_rows, heads_here), jnp.float32),
            pltpu.VMEM((text_rows, heads_here), jnp.float32),
            pltpu.VMEM((text_rows, heads_here), jnp.bfloat16),
            pltpu.VMEM((2, 8, text_rows, heads_here), jnp.bfloat16),
            pltpu.VMEM((2 * COLUMNS, 2, text_rows, heads_here), jnp.bfloat16),
            pltpu.VMEM((SLOTS, SOURCES, tokens, HEAD_DIM), jnp.bfloat16),
            pltpu.VMEM((2, 8, 128), jnp.float32),
            pltpu.VMEM(prompt_embed.shape, jnp.bfloat16),
            pltpu.VMEM(key_weight.shape, jnp.bfloat16),
            pltpu.VMEM(value_weight.shape, jnp.bfloat16),
            pltpu.VMEM((8, tokens, heads_here), jnp.bfloat16),
            pltpu.VMEM((8, tokens, heads_here), jnp.bfloat16),
            pltpu.VMEM((tokens, width), jnp.bfloat16),
            pltpu.VMEM((tokens, width), jnp.bfloat16),
            dma((SLOTS,)),
            dma((SLOTS,)),
            dma((2, SLOTS, 2)),
            dma((2, SLOTS)),
            dma((2, SLOTS)),
            dma((SLOTS,)),
            dma,
            dma((7,)),
            dma((7,)),
            dma((3,)),
        ],
        compiler_params=pltpu.CompilerParams(
            collective_id=0, has_side_effects=True, vmem_limit_bytes=63 * 1024 * 1024
        ),
    )(
        queries[0],
        key_rows[0],
        value_rows[0],
        text_queries[0],
        prompt_embed,
        key_weight,
        value_weight,
        stop_count,
        prompt_length,
    )
    return mixed[None]


def solution(mesh):
    placed = (
        P("blk", ("head", "enc"), None),
        P("blk", ("head", "enc"), None),
        P("blk", ("head", "enc"), None),
        P("blk", ("head", "enc"), None),
        P("enc", "blk"),
        P("blk", "head"),
        P("blk", "head"),
        P("blk"),
        P(),
    )
    return jax.shard_map(
        body, mesh=mesh, in_specs=placed, out_specs=P("blk", ("head", "enc"), None), check_vma=False
    )
```

time: 163 us -> 148 us (0.908)
  Pallas kernels: 153 us -> 145 us
  local copies, waits for them, and re-layouts: 7.71 us -> 1.91 us
    pallas_call x1, Pallas kernels: 153 us -> 145 us  [body(): pl.pallas_call(kernel, out_shape=jax.ShapeDtypeStruct((tokens, width), jn...]
    unnamed x15 -> x1, local copies, waits for them, and re-layouts: 7.71 us -> 1.91 us
where the time goes in v2:
time: 148 us
  Pallas kernels  145 us (98%)
  local copies, waits for them, and re-layouts  1.91 us (1%)
    pallas_call x1, Pallas kernels, body(): pl.pallas_call(kernel, out_shape=jax.ShapeDtypeStruct((tokens, width), jn...  145 us

profile of v2, /device:TPU:1, one launch (start us, length us, event | category | flops | bytes accessed | tf_op | source)
XLA Modules:
  0.0 147.9 jit_solution(12622378332820748024)
XLA Ops:
  1.3 144.7 %shard_map.91 = bf16[56,5120]{1,0:T(8,128)(2,1)} custom-call(bf16[56,5120]{1,0:T(8,128)(2,1)} %bitcast.6, bf16[56,5120]{1,0:T(8,128)(2,1)} %bitcast.7, bf16[56,5120]{1,0:T(8,128)(2,1)} %bitcast.8, bf16[56,5120]{1,0:T(8,128)(2,1)} %bitcast.9, bf16[256,128]{1,0:T(8,128)(2,1)} %emb_hbm.1, bf16[128,640]{1,0:T(8,128)(2,1)} %wk_hbm.1, bf16[128,640]{1,0:T(8,128)(2,1)} %wv_hbm.1, ...), custom_call_target="tpu_custom_call" | custom-call | tf_op jit(solution)/shard_map/pallas_call | solution.py:412
  146.0 1.9 %copy.13 = bf16[1,56,5120]{2,1,0:T(8,128)(2,1)} copy(bf16[1,56,5120]{2,1,0:T(8,128)(2,1)} %bitcast.5) | data formatting | bytes 1146880

commit v3 on v2

--- a/solution.py
+++ b/solution.py
@@ -286,18 +286,19 @@
             mix = jnp.dot(weights.astype(jnp.bfloat16), text_values, preferred_element_type=jnp.float32)
             mix = mix / jnp.sum(weights, axis=1, keepdims=True)
             cross_out[:, :, cols] = mix.reshape(8, tokens, HEAD_DIM).astype(jnp.bfloat16)
-            return 0
-
-        def answer(n, _):
-            to = (mine5 + n) % 8
-            place = cross_mix.at[:, pl.ds(pl.multiple_of(mine5 * lot, HEAD_DIM), lot)]
-            give(n == 0, cross_out.at[to], place, ANSWER, beside((to // 2) * 4 + y, to % 2))
+            place = cross_mix.at[:, pl.ds(pl.multiple_of(mine5 * lot + h * HEAD_DIM, HEAD_DIM), HEAD_DIM)]
+
+            def answer(n, _):
+                to = (mine5 + n) % 8
+                give(n == 0, cross_out.at[to, :, cols], place, ANSWER, beside((to // 2) * 4 + y, to % 2))
+                return 0
+
+            lax.fori_loop(0, 8, answer, 0)
             return 0
 
         wait_for(cross_in, t_recv.at[ASK])
         wait_for(text, t_recv.at[ROWS])
         lax.fori_loop(0, 5, head, 0)
-        lax.fori_loop(0, 8, answer, 0)
 
     def attend(hs):
         def block(i, _):

time: 148 us -> 146 us (0.986)
  Pallas kernels: 145 us -> 142 us
    pallas_call x1, Pallas kernels: 145 us -> 142 us  [body(): pl.pallas_call(kernel, out_shape=jax.ShapeDtypeStruct((tokens, width), jn...]
where the time goes in v3:
time: 146 us; the launch traced here: 145 us
  Pallas kernels  142 us (97%)
  local copies, waits for them, and re-layouts  1.91 us (1%)
    pallas_call x1, Pallas kernels, body(): pl.pallas_call(kernel, out_shape=jax.ShapeDtypeStruct((tokens, width), jn...  142 us

profile of v3, /device:TPU:1, one launch (start us, length us, event | category | flops | bytes accessed | tf_op | source)
XLA Modules:
  0.0 145.5 jit_solution(7938588318452644239)
XLA Ops:
  1.3 142.2 %shard_map.91 = bf16[56,5120]{1,0:T(8,128)(2,1)} custom-call(bf16[56,5120]{1,0:T(8,128)(2,1)} %bitcast.6, bf16[56,5120]{1,0:T(8,128)(2,1)} %bitcast.7, bf16[56,5120]{1,0:T(8,128)(2,1)} %bitcast.8, bf16[56,5120]{1,0:T(8,128)(2,1)} %bitcast.9, bf16[256,128]{1,0:T(8,128)(2,1)} %emb_hbm.1, bf16[128,640]{1,0:T(8,128)(2,1)} %wk_hbm.1, bf16[128,640]{1,0:T(8,128)(2,1)} %wv_hbm.1, ...), custom_call_target="tpu_custom_call" | custom-call | tf_op jit(solution)/shard_map/pallas_call | solution.py:413
  143.5 1.9 %copy.13 = bf16[1,56,5120]{2,1,0:T(8,128)(2,1)} copy(bf16[1,56,5120]{2,1,0:T(8,128)(2,1)} %bitcast.5) | data formatting | bytes 1146880

commit v4 on v3

--- a/solution.py
+++ b/solution.py
@@ -155,14 +155,14 @@
         else:
             run()
 
-    def forward(hs, m):
+    def forward(hs, m, i):
         next_c = (c + 1) % COLUMNS
         next_e = jnp.where(c == COLUMNS - 1, 1 - e, e)
         return pltpu.make_async_remote_copy(
-            src_ref=kv.at[m, hs],
-            dst_ref=kv.at[m + 1, hs],
-            send_sem=fwd_send.at[m, hs],
-            recv_sem=fwd_recv.at[m, hs],
+            src_ref=kv.at[m, hs, i],
+            dst_ref=kv.at[m + 1, hs, i],
+            send_sem=fwd_send.at[m, hs, i],
+            recv_sem=fwd_recv.at[m, hs, i],
             device_id=(g, p * COLUMNS + next_c, next_e),
             device_id_type=MESH,
         )
@@ -173,14 +173,15 @@
             for i in range(2):
                 whole = kv_in[hs, i].astype(jnp.float32).reshape(rows, HEAD_DIM)
                 kv[0, hs, i] = whole.astype(jnp.bfloat16)
-            forward(hs, 0).start()
+                forward(hs, 0, i).start()
 
         per_slot(hs, run)
 
     def keys_pass(hs):
         def run():
-            forward(hs, 0).wait_recv()
-            forward(hs, 1).start()
+            for i in range(2):
+                forward(hs, 0, i).wait_recv()
+                forward(hs, 1, i).start()
 
         per_slot(hs, run)
 
@@ -345,7 +346,8 @@
 
         def run():
             wait_for(q_in.at[hs], q_recv.at[hs])
-            forward(hs, 1).wait_recv()
+            for i in range(2):
+                forward(hs, 1, i).wait_recv()
             lax.fori_loop(0, SOURCES // group, block, 0)
 
         per_slot(hs, run)
@@ -378,8 +380,9 @@
     for hs in range(SLOTS):
 
         def finish(hs=hs):
-            forward(hs, 0).wait_send()
-            forward(hs, 1).wait_send()
+            for m in range(2):
+                for i in range(2):
+                    forward(hs, m, i).wait_send()
 
             @pl.when(home)
             def _():
@@ -439,8 +442,8 @@
             dma((SLOTS,)),
             dma((SLOTS,)),
             dma((2, SLOTS, 2)),
-            dma((2, SLOTS)),
-            dma((2, SLOTS)),
+            dma((2, SLOTS, 2)),
+            dma((2, SLOTS, 2)),
             dma((SLOTS,)),
             dma,
             dma((7,)),

time: 146 us -> 146 us (level)
  no operation moved by 1% of the time
where the time goes in v4:
time: 146 us
  Pallas kernels  142 us (97%)
  local copies, waits for them, and re-layouts  1.91 us (1%)
    pallas_call x1, Pallas kernels, body(): pl.pallas_call(kernel, out_shape=jax.ShapeDtypeStruct((tokens, width), jn...  142 us

profile of v4, /device:TPU:1, one launch (start us, length us, event | category | flops | bytes accessed | tf_op | source)
XLA Modules:
  0.0 145.5 jit_solution(892107273491499400)
XLA Ops:
  1.3 142.3 %shard_map.91 = bf16[56,5120]{1,0:T(8,128)(2,1)} custom-call(bf16[56,5120]{1,0:T(8,128)(2,1)} %bitcast.6, bf16[56,5120]{1,0:T(8,128)(2,1)} %bitcast.7, bf16[56,5120]{1,0:T(8,128)(2,1)} %bitcast.8, bf16[56,5120]{1,0:T(8,128)(2,1)} %bitcast.9, bf16[256,128]{1,0:T(8,128)(2,1)} %emb_hbm.1, bf16[128,640]{1,0:T(8,128)(2,1)} %wk_hbm.1, bf16[128,640]{1,0:T(8,128)(2,1)} %wv_hbm.1, ...), custom_call_target="tpu_custom_call" | custom-call | tf_op jit(solution)/shard_map/pallas_call | solution.py:416
  143.6 1.9 %copy.13 = bf16[1,56,5120]{2,1,0:T(8,128)(2,1)} copy(bf16[1,56,5120]{2,1,0:T(8,128)(2,1)} %bitcast.5) | data formatting | bytes 1146880
